TPU v7x, 32 devices: a whole 2x2x4 slice. The times are simulated.
32 devices in a mesh: dp: 2 (over x), expert: 16 (over z, y, core).
Axes of the slice: x: 2, y: 2, z: 4, core: 2. Of those that a mesh axis runs over, the one named last changes fastest.
Arguments:
- tokens: bfloat16 [4096, 1536], P(('dp', 'expert')), may hold values from -6 to 6
- cotangent: bfloat16 [4096, 1536], P(('dp', 'expert')), may hold values from -6 to 6
- norm_attn: bfloat16 [1536], P(('dp', 'expert')), may hold values from 0.5 to 1.5
- w_query: bfloat16 [1536, 1536], P(('dp', 'expert')), may hold values from -0.15625 to 0.15625
- key_projection: bfloat16 [1536, 512], P(('dp', 'expert')), may hold values from -0.15625 to 0.15625
- value_projection: bfloat16 [1536, 512], P(('dp', 'expert')), may hold values from -0.15625 to 0.15625
- w_out: bfloat16 [1536, 1536], P(('dp', 'expert')), may hold values from -0.625 to 0.625
- norm_ffn: bfloat16 [1536], P(('dp', 'expert')), may hold values from 0.5 to 1.5
- w_router: bfloat16 [1536, 16], P(('dp', 'expert')), may hold values from -0.078125 to 0.078125
- expert_gate: bfloat16 [16, 1536, 512], P('expert', 'dp'), may hold values from -0.15625 to 0.15625
- expert_up: bfloat16 [16, 1536, 512], P('expert', 'dp'), may hold values from -0.15625 to 0.15625
- expert_down: bfloat16 [16, 512, 1536], P('expert', None, 'dp'), may hold values from -0.75 to 0.75
- routes: int32 [4096, 8], P(('dp', 'expert')), may hold values from 0 to 15, all different within a row
- slot_order: int32 [32, 1024], P(('dp', 'expert')), may hold values from 0 to 1023, each once within a row
- doc_lengths: int32 [16, 3], P('expert'), may hold values from 1 to 224, 256 in all within a row
- deal: int32 [2, 16, 128], P(None, 'expert'), may hold values from 0 to 255, as said below
Outputs:
- output: bfloat16 [4096, 1536], P(('dp', 'expert'))
- tokens_grad: bfloat16 [4096, 1536], P(('dp', 'expert'))
- norm_attn_grad: float32 [1536], P(('dp', 'expert'))
- w_query_grad: float32 [1536, 1536], P(('dp', 'expert'))
- w_key_grad: float32 [1536, 512], P(('dp', 'expert'))
- w_value_grad: float32 [1536, 512], P(('dp', 'expert'))
- w_out_grad: float32 [1536, 1536], P(('dp', 'expert'))
- norm_ffn_grad: float32 [1536], P(('dp', 'expert'))
- w_router_grad: float32 [1536, 16], P(('dp', 'expert'))
- expert_gate_grad: float32 [16, 1536, 512], P('expert', 'dp')
- expert_up_grad: float32 [16, 1536, 512], P('expert', 'dp')
- expert_down_grad: float32 [16, 512, 1536], P('expert', None, 'dp')
Inputs may be any that keep to these rules, and one draw needn't show every extreme that they name: `routes`: the 8 experts of one token are different. `slot_order`: each row lists every number 0 to 1023 once. `doc_lengths`: each row sums to 256; its longest document has 224 tokens. Cut the places of a group into 4 pieces of 64 consecutive places; deal[i, e] lists, in rising order, the places of piece p and of piece 2 * 2 - 1 - p, where p differs over i for each e (so the 2 entries deal[i, e] together list every place once).
All inputs are finite; a program needn't handle non-finite values.
Results may differ from a plain program's by a relative error of at most 0.017.
Values may be sent and summed in bfloat16 or wider, within the bound.
A program may use at most 192 MiB of HBM per device.

v0:
```python
import math

import jax
import jax.numpy as jnp
from jax import lax
from jax.sharding import PartitionSpec as P

HEAD_DIM = 64


NORM_EPS = 1e-05
MASK_FILL = -1e30
ROPE_BASE = 10000.0


def dot_plain(left_side, right_side):
    return jnp.dot(left_side, right_side, preferred_element_type=jnp.float32)


def dot_last(left_side, right_side):
    return lax.dot_general(
        left_side, right_side, (((1,), (1,)), ((), ())), preferred_element_type=jnp.float32
    )


def dot_first(left_side, right_side):
    return lax.dot_general(
        left_side, right_side, (((0,), (0,)), ((), ())), preferred_element_type=jnp.float32
    )


def doc_layout(lengths, places):
    doc_ends = jnp.cumsum(lengths)
    doc_starts = doc_ends - lengths
    doc_ids = jnp.sum((places[:, None] >= doc_ends[None, :]).astype(jnp.int32), axis=1)
    member = doc_ids[:, None] == jnp.arange(lengths.shape[0], dtype=jnp.int32)[None, :]
    offsets = places - jnp.sum(jnp.where(member, doc_starts[None, :], 0), axis=1)
    return (doc_ids, offsets)


def rope_tables(offsets, head_size):
    half_size = head_size // 2
    frequency = ROPE_BASE ** (-2.0 * jnp.arange(half_size, dtype=jnp.float32) / head_size)
    angles = offsets.astype(jnp.float32)[:, None] * frequency[None, :]
    return (jnp.cos(angles), jnp.sin(angles))


def apply_rotation(values, cosine_lookup, sine_lookup):
    half_size = values.shape[-1] // 2
    first_half = values[..., :half_size]
    second = values[..., half_size:]
    cos_rows = cosine_lookup[:, None, :]
    sin_rows = sine_lookup[:, None, :]
    return jnp.concatenate(
        [first_half * cos_rows - second * sin_rows, second * cos_rows + first_half * sin_rows],
        axis=-1,
    )


def unrotate(gradient, cosine_lookup, sine_lookup):
    half_size = gradient.shape[-1] // 2
    first_half = gradient[..., :half_size]
    second = gradient[..., half_size:]
    cos_rows = cosine_lookup[:, None, :]
    sin_rows = sine_lookup[:, None, :]
    return jnp.concatenate(
        [first_half * cos_rows + second * sin_rows, second * cos_rows - first_half * sin_rows],
        axis=-1,
    )


def assign_slots(routes, take_order, experts, capacity):
    count_of_rows, top_count = routes.shape
    flat_routes = routes.reshape(-1)
    chosen = flat_routes[take_order]
    expert_hits = (chosen[:, None] == jnp.arange(experts, dtype=jnp.int32)[None, :]).astype(
        jnp.int32
    )
    slot_rank = jnp.sum(jnp.cumsum(expert_hits, axis=0) * expert_hits, axis=1) - 1
    slot_index = jnp.where(slot_rank < capacity, chosen * capacity + slot_rank, experts * capacity)
    pair_slot = jnp.zeros((flat_routes.shape[0],), jnp.int32).at[take_order].set(slot_index)
    slot_token = (
        jnp.full((experts * capacity + 1,), count_of_rows, jnp.int32)
        .at[slot_index]
        .set(take_order // top_count)
    )
    return (pair_slot, slot_token[: experts * capacity])


def body(
    tokens,
    cotangent,
    norm_attn,
    w_query,
    key_projection,
    value_projection,
    w_out,
    norm_ffn,
    w_router,
    expert_gate,
    expert_up,
    expert_down,
    routes,
    slot_order,
    doc_lengths,
    deal,
):
    gain_attn, full_query, gathered_key, gathered_value, full_out, gain_ffn, full_router = (
        lax.all_gather(norm_attn, ("dp", "expert"), axis=0, tiled=True),
        lax.all_gather(w_query, ("dp", "expert"), axis=0, tiled=True),
        lax.all_gather(key_projection, ("dp", "expert"), axis=0, tiled=True),
        lax.all_gather(value_projection, ("dp", "expert"), axis=0, tiled=True),
        lax.all_gather(w_out, ("dp", "expert"), axis=0, tiled=True),
        lax.all_gather(norm_ffn, ("dp", "expert"), axis=0, tiled=True),
        lax.all_gather(w_router, ("dp", "expert"), axis=0, tiled=True),
    )
    full_gate, full_up, full_down = (
        lax.all_gather(expert_gate[0], "dp", axis=0, tiled=True),
        lax.all_gather(expert_up[0], "dp", axis=0, tiled=True),
        lax.all_gather(expert_down[0], "dp", axis=1, tiled=True),
    )
    count_of_rows, model_width = tokens.shape
    top_count = routes.shape[1]
    experts = full_router.shape[1]
    owners = lax.axis_size("expert")
    capacity = 9 * count_of_rows * top_count // (8 * experts)
    head_count = full_query.shape[1] // HEAD_DIM
    groups = gathered_key.shape[1] // HEAD_DIM
    head_ratio = head_count // groups
    scale_attn = gain_attn.astype(jnp.float32)
    scale_ffn = gain_ffn.astype(jnp.float32)
    score_scale = HEAD_DIM ** (-0.5)
    group_places = deal[:, 0, :].reshape(-1)
    group_docs, group_offsets = doc_layout(doc_lengths[0], group_places)
    shard_start = lax.axis_index("dp") * count_of_rows
    places = lax.dynamic_slice_in_dim(group_places, shard_start, count_of_rows)
    doc_ids = lax.dynamic_slice_in_dim(group_docs, shard_start, count_of_rows)
    offsets = lax.dynamic_slice_in_dim(group_offsets, shard_start, count_of_rows)
    cosine_lookup, sine_lookup = rope_tables(offsets, HEAD_DIM)
    inputs = tokens.astype(jnp.float32)
    inverse_one = lax.rsqrt(jnp.mean(inputs * inputs, axis=1, keepdims=True) + NORM_EPS)
    normed_one = inputs * inverse_one
    attention_input = (normed_one * scale_attn).astype(jnp.bfloat16)
    query_rows = apply_rotation(
        dot_plain(attention_input, full_query).reshape(count_of_rows, head_count, HEAD_DIM),
        cosine_lookup,
        sine_lookup,
    ).astype(jnp.bfloat16)
    key_matrix_rows = apply_rotation(
        dot_plain(attention_input, gathered_key).reshape(count_of_rows, groups, HEAD_DIM),
        cosine_lookup,
        sine_lookup,
    ).astype(jnp.bfloat16)
    value_matrix_rows = dot_plain(attention_input, gathered_value).astype(jnp.bfloat16)
    all_keys, all_values = (
        lax.all_gather(key_matrix_rows.reshape(count_of_rows, -1), "dp", axis=0, tiled=True),
        lax.all_gather(value_matrix_rows, "dp", axis=0, tiled=True),
    )
    group_rows = all_keys.shape[0]
    key_span = math.gcd(group_rows, 512)
    span_count = group_rows // key_span
    key_spans = (
        all_keys.reshape(span_count, key_span, groups, HEAD_DIM),
        all_values.reshape(span_count, key_span, groups, HEAD_DIM),
        group_places.reshape(span_count, key_span),
        group_docs.reshape(span_count, key_span),
    )
    grouped_q = query_rows.reshape(count_of_rows, groups, head_ratio, HEAD_DIM)

    def span_scores(key_block, key_place, key_doc):
        visible = (doc_ids[:, None] == key_doc[None, :]) & (places[:, None] >= key_place[None, :])
        scores = (
            jnp.einsum("qgrd,kgd->grqk", grouped_q, key_block, preferred_element_type=jnp.float32)
            * score_scale
        )
        return jnp.where(visible[None, None], scores, MASK_FILL)

    def extent(carry, operands):
        run_max, run_sum = carry
        key_block, value_block, key_place, key_doc = operands
        scores = span_scores(key_block, key_place, key_doc)
        new_max = jnp.maximum(run_max, jnp.max(scores, axis=-1, keepdims=True))
        run_sum = run_sum * jnp.exp(run_max - new_max) + jnp.sum(
            jnp.exp(scores - new_max), axis=-1, keepdims=True
        )
        return ((new_max, run_sum), None)

    stat_shape = (groups, head_ratio, count_of_rows, 1)
    (row_max, row_sum), _ = lax.scan(
        extent,
        (jnp.full(stat_shape, MASK_FILL, jnp.float32), jnp.zeros(stat_shape, jnp.float32)),
        key_spans,
    )
    log_total = row_max + jnp.log(row_sum)

    def weigh_values(running, operands):
        key_block, value_block, key_place, key_doc = operands
        weights = jnp.exp(span_scores(key_block, key_place, key_doc) - log_total).astype(
            jnp.bfloat16
        )
        return (
            running
            + jnp.einsum(
                "grqk,kgd->qgrd", weights, value_block, preferred_element_type=jnp.float32
            ),
            None,
        )

    attended, _ = lax.scan(
        weigh_values,
        jnp.zeros((count_of_rows, groups, head_ratio, HEAD_DIM), jnp.float32),
        key_spans,
    )
    attended = attended.reshape(count_of_rows, head_count * HEAD_DIM).astype(jnp.bfloat16)
    hidden_state = inputs + dot_plain(attended, full_out)
    inverse_two = lax.rsqrt(jnp.mean(hidden_state * hidden_state, axis=1, keepdims=True) + NORM_EPS)
    normed_two = hidden_state * inverse_two
    ffn_in = (normed_two * scale_ffn).astype(jnp.bfloat16)
    logits = dot_plain(ffn_in, full_router)
    route_hits = (routes[:, :, None] == jnp.arange(experts, dtype=jnp.int32)[None, None, :]).astype(
        jnp.float32
    )
    chosen = jnp.sum(route_hits * logits[:, None, :], axis=-1)
    gate_values = jax.nn.softmax(chosen, axis=-1)
    pair_slot, slot_token = assign_slots(routes, slot_order[0], experts, capacity)
    padded_in = jnp.concatenate([ffn_in, jnp.zeros((1, model_width), jnp.bfloat16)], axis=0)
    outgoing = padded_in[slot_token].reshape(owners, capacity, model_width)
    arrived = lax.all_to_all(outgoing, "expert", split_axis=0, concat_axis=0, tiled=True)
    flat_rows = arrived.reshape(-1, model_width)
    gate_pre = dot_plain(flat_rows, full_gate)
    up_pre = dot_plain(flat_rows, full_up)
    hidden = (jax.nn.silu(gate_pre) * up_pre).astype(jnp.bfloat16)
    result = dot_plain(hidden, full_down).astype(jnp.bfloat16).reshape(arrived.shape)
    sent_back = lax.all_to_all(result, "expert", split_axis=0, concat_axis=0, tiled=True)
    exchanged = (
        sent_back,
        arrived,
        gate_pre.reshape(arrived.shape[0], arrived.shape[1], -1),
        up_pre.reshape(arrived.shape[0], arrived.shape[1], -1),
    )
    returned = exchanged[0]
    expert_rows = exchanged[1].reshape(-1, model_width)
    gate_pre = exchanged[2].reshape(expert_rows.shape[0], -1)
    up_pre = exchanged[3].reshape(expert_rows.shape[0], -1)
    out_grad = cotangent.astype(jnp.float32)
    padded_back = jnp.concatenate(
        [returned.reshape(-1, model_width), jnp.zeros((1, model_width), jnp.bfloat16)], axis=0
    )
    slot_grid = pair_slot.reshape(count_of_rows, top_count)
    mixture = jnp.zeros((count_of_rows, model_width), jnp.float32)
    gate_parts = []
    for column in range(top_count):
        picked = padded_back[slot_grid[:, column]].astype(jnp.float32)
        mixture = mixture + gate_values[:, column : column + 1] * picked
        gate_parts.append(jnp.sum(out_grad * picked, axis=1))
    output = (hidden_state + mixture).astype(jnp.bfloat16)
    gate_grad = jnp.stack(gate_parts, axis=1)
    slot_gate = (
        jnp.zeros((experts * capacity + 1,), jnp.float32)
        .at[pair_slot]
        .set(gate_values.reshape(-1))[: experts * capacity]
    )
    padded_grad = jnp.concatenate([out_grad, jnp.zeros((1, model_width), jnp.float32)], axis=0)
    slot_grad = (
        (slot_gate[:, None] * padded_grad[slot_token])
        .astype(jnp.bfloat16)
        .reshape(owners, capacity, model_width)
    )
    arrived_grad = lax.all_to_all(
        slot_grad, "expert", split_axis=0, concat_axis=0, tiled=True
    ).reshape(-1, model_width)
    sigmoid_gate = jax.nn.sigmoid(gate_pre)
    silu_gate = gate_pre * sigmoid_gate
    hidden = (silu_gate * up_pre).astype(jnp.bfloat16)
    hidden_grad = dot_last(arrived_grad, full_down)
    gate_pre_grad = (
        hidden_grad * up_pre * sigmoid_gate * (1.0 + gate_pre * (1.0 - sigmoid_gate))
    ).astype(jnp.bfloat16)
    up_pre_grad = (hidden_grad * silu_gate).astype(jnp.bfloat16)
    down_weight_grad = dot_first(hidden, arrived_grad)
    gate_weight_grad = dot_first(expert_rows, gate_pre_grad)
    up_weight_grad = dot_first(expert_rows, up_pre_grad)
    row_grad = (dot_last(gate_pre_grad, full_gate) + dot_last(up_pre_grad, full_up)).astype(
        jnp.bfloat16
    )
    token_rows_grad = lax.all_to_all(
        row_grad.reshape(owners, capacity, model_width),
        "expert",
        split_axis=0,
        concat_axis=0,
        tiled=True,
    )
    gate_summed, up_summed, down_summed = (
        lax.psum_scatter(
            gate_weight_grad.astype(jnp.bfloat16), "dp", scatter_dimension=0, tiled=True
        ).astype(jnp.float32),
        lax.psum_scatter(
            up_weight_grad.astype(jnp.bfloat16), "dp", scatter_dimension=0, tiled=True
        ).astype(jnp.float32),
        lax.psum_scatter(
            down_weight_grad.astype(jnp.bfloat16), "dp", scatter_dimension=1, tiled=True
        ).astype(jnp.float32),
    )
    dispatch_grad = jax.ops.segment_sum(
        token_rows_grad.reshape(-1, model_width).astype(jnp.float32),
        slot_token,
        num_segments=count_of_rows + 1,
    )[:count_of_rows]
    chosen_grad = gate_values * (
        gate_grad - jnp.sum(gate_values * gate_grad, axis=1, keepdims=True)
    )
    logit_grad = jnp.sum(route_hits * chosen_grad[:, :, None], axis=1).astype(jnp.bfloat16)
    router_grad = dot_first(ffn_in, logit_grad)
    ffn_grad = dispatch_grad + dot_last(logit_grad, full_router)
    ffn_gain_grad = jnp.sum(ffn_grad * normed_two, axis=0)
    scaled_two = ffn_grad * scale_ffn
    state_grad = out_grad + inverse_two * (
        scaled_two - normed_two * jnp.mean(scaled_two * normed_two, axis=1, keepdims=True)
    )
    branch_grad = state_grad.astype(jnp.bfloat16)
    out_weight_grad = dot_first(attended, branch_grad)
    attended_grad = (
        dot_last(branch_grad, full_out)
        .astype(jnp.bfloat16)
        .reshape(count_of_rows, groups, head_ratio, HEAD_DIM)
    )

    def spread_sum(running, operands):
        key_block, value_block, key_place, key_doc = operands
        probs = jnp.exp(span_scores(key_block, key_place, key_doc) - log_total)
        prob_grad = jnp.einsum(
            "qgrd,kgd->grqk", attended_grad, value_block, preferred_element_type=jnp.float32
        )
        return (running + jnp.sum(probs * prob_grad, axis=-1, keepdims=True), None)

    score_shift, _ = lax.scan(spread_sum, jnp.zeros(stat_shape, jnp.float32), key_spans)

    def back_span(running, operands):
        key_block, value_block, key_place, key_doc = operands
        probs = jnp.exp(span_scores(key_block, key_place, key_doc) - log_total)
        prob_grad = jnp.einsum(
            "qgrd,kgd->grqk", attended_grad, value_block, preferred_element_type=jnp.float32
        )
        score_grad = (probs * (prob_grad - score_shift)).astype(jnp.bfloat16)
        running = running + jnp.einsum(
            "grqk,kgd->qgrd", score_grad, key_block, preferred_element_type=jnp.float32
        )
        key_part = (
            jnp.einsum("grqk,qgrd->kgd", score_grad, grouped_q, preferred_element_type=jnp.float32)
            * score_scale
        )
        value_part = jnp.einsum(
            "grqk,qgrd->kgd",
            probs.astype(jnp.bfloat16),
            attended_grad,
            preferred_element_type=jnp.float32,
        )
        return (running, (key_part.reshape(key_span, -1), value_part.reshape(key_span, -1)))

    query_sum, (key_parts, value_parts) = lax.scan(
        back_span, jnp.zeros((count_of_rows, groups, head_ratio, HEAD_DIM), jnp.float32), key_spans
    )
    key_grad, value_sum = (
        lax.psum_scatter(
            key_parts.reshape(group_rows, -1).astype(jnp.bfloat16),
            "dp",
            scatter_dimension=0,
            tiled=True,
        ).astype(jnp.float32),
        lax.psum_scatter(
            value_parts.reshape(group_rows, -1).astype(jnp.bfloat16),
            "dp",
            scatter_dimension=0,
            tiled=True,
        ).astype(jnp.float32),
    )
    query_grad = query_sum * score_scale
    query_lin_grad = unrotate(
        query_grad.reshape(count_of_rows, head_count, HEAD_DIM), cosine_lookup, sine_lookup
    )
    query_lin_grad = query_lin_grad.reshape(count_of_rows, -1).astype(jnp.bfloat16)
    key_lin_grad = (
        unrotate(key_grad.reshape(count_of_rows, groups, HEAD_DIM), cosine_lookup, sine_lookup)
        .reshape(count_of_rows, -1)
        .astype(jnp.bfloat16)
    )
    value_lin_grad = value_sum.astype(jnp.bfloat16)
    query_weight_grad = dot_first(attention_input, query_lin_grad)
    key_weight_grad = dot_first(attention_input, key_lin_grad)
    value_weight_grad = dot_first(attention_input, value_lin_grad)
    attn_grad = (
        dot_last(query_lin_grad, full_query)
        + dot_last(key_lin_grad, gathered_key)
        + dot_last(value_lin_grad, gathered_value)
    )
    attn_gain_grad = jnp.sum(attn_grad * normed_one, axis=0)
    scaled_one = attn_grad * scale_attn
    tokens_grad = (
        state_grad
        + inverse_one
        * (scaled_one - normed_one * jnp.mean(scaled_one * normed_one, axis=1, keepdims=True))
    ).astype(jnp.bfloat16)
    summed = (
        lax.psum_scatter(attn_gain_grad, ("dp", "expert"), scatter_dimension=0, tiled=True),
        lax.psum_scatter(query_weight_grad, ("dp", "expert"), scatter_dimension=0, tiled=True),
        lax.psum_scatter(key_weight_grad, ("dp", "expert"), scatter_dimension=0, tiled=True),
        lax.psum_scatter(value_weight_grad, ("dp", "expert"), scatter_dimension=0, tiled=True),
        lax.psum_scatter(out_weight_grad, ("dp", "expert"), scatter_dimension=0, tiled=True),
        lax.psum_scatter(ffn_gain_grad, ("dp", "expert"), scatter_dimension=0, tiled=True),
        lax.psum_scatter(router_grad, ("dp", "expert"), scatter_dimension=0, tiled=True),
    )
    return (
        output,
        tokens_grad,
        summed[0],
        summed[1],
        summed[2],
        summed[3],
        summed[4],
        summed[5],
        summed[6],
        gate_summed[None],
        up_summed[None],
        down_summed[None],
    )


def solution(mesh):
    in_specs = (
        P(("dp", "expert"), None),
        P(("dp", "expert"), None),
        P(("dp", "expert")),
        P(("dp", "expert"), None),
        P(("dp", "expert"), None),
        P(("dp", "expert"), None),
        P(("dp", "expert"), None),
        P(("dp", "expert")),
        P(("dp", "expert"), None),
        P("expert", "dp", None),
        P("expert", "dp", None),
        P("expert", None, "dp"),
        P(("dp", "expert"), None),
        P(("dp", "expert"), None),
        P("expert", None),
        P(None, "expert", None),
    )
    out_specs = (
        P(("dp", "expert"), None),
        P(("dp", "expert"), None),
        P(("dp", "expert")),
        P(("dp", "expert"), None),
        P(("dp", "expert"), None),
        P(("dp", "expert"), None),
        P(("dp", "expert"), None),
        P(("dp", "expert")),
        P(("dp", "expert"), None),
        P("expert", "dp", None),
        P("expert", "dp", None),
        P("expert", None, "dp"),
    )
    return jax.shard_map(body, mesh=mesh, in_specs=in_specs, out_specs=out_specs, check_vma=False)
```

profile of v0, /device:TPU:24, one launch (start us, length us, event | category | flops | bytes accessed | tf_op | source)
XLA Modules:
  0.0 1456.2 jit_solution(2097863261783350576)
XLA Ops:
  16.4 39.3 %all-reduce.8 = (bf16[1536]{0:T(1024)(128)(2,1)S(1)}, bf16[1536]{0:T(1024)(128)(2,1)S(1)}) all-reduce(bf16[1536]{0:T(1024)(128)(2,1)S(1)} %dynamic-update-slice, bf16[1536]{0:T(1024)(128)(2,1)S(1)} %dynamic-update-slice.1), channel_id=1, replica_groups=mesh['dp'=2,'expert'=16] {'dp','expert'}, use_global_device_ids=true, to_apply=%add.3 | all-reduce | flops 3072 | bytes 12288
  79.7 44.1 %all-gather.14.cloned.1.call-done = bf16[1536,512]{1,0:T(8,128)(2,1)} async-done(((bf16[48,512]{1,0:T(8,128)(2,1)}), bf16[1536,512]{1,0:T(8,128)(2,1)}) %all-gather.14.cloned.1.call-update) | async-done | bytes 1572880 | tf_op jit(solution)/shard_map/all_gather | solution.py:111
  126.0 6.4 all_gather.40
  132.4 56.6 %all-gather.16.cloned.1.call-done = bf16[1536,1536]{1,0:T(8,128)(2,1)} async-done(((bf16[48,1536]{1,0:T(8,128)(2,1)}), bf16[1536,1536]{1,0:T(8,128)(2,1)}) %all-gather.16.cloned.1.call-update) | async-done | bytes 4718608 | tf_op jit(solution)/shard_map/all_gather | solution.py:110
  196.4 57.7 %all-gather.18.cloned.1.call-done = bf16[1536,1536]{1,0:T(8,128)(2,1)} async-done(((bf16[48,1536]{1,0:T(8,128)(2,1)}), bf16[1536,1536]{1,0:T(8,128)(2,1)}) %all-gather.18.cloned.1.call-update) | async-done | bytes 4718608 | tf_op jit(solution)/shard_map/all_gather | solution.py:113
  262.9 6.0 all-to-all-start
  270.6 28.2 %all-gather.20.cloned.1.call-done = bf16[1,1536,512]{2,1,0:T(8,128)(2,1)} async-done(((bf16[1,768,512]{2,1,0:T(8,128)(2,1)}), bf16[1,1536,512]{2,1,0:T(8,128)(2,1)}) %all-gather.20.cloned.1.call-update) | async-done | bytes 1572880 | tf_op jit(solution)/shard_map/all_gather | solution.py:118
  298.8 42.6 %all-to-all-done = bf16[16,72,1536]{2,1,0:T(8,128)(2,1)} async-done(((bf16[16,72,1536]{2,1,0:T(8,128)(2,1)}), bf16[16,72,1536]{2,1,0:T(8,128)(2,1)}, u32[]{:S(2)}, u32[]{:S(2)}) %all-to-all-start) | async-done | bytes 3538976 | tf_op jit(solution)/shard_map/all_to_all | solution.py:228
  347.4 7.2 multiply_convert_fusion.3
  361.5 9.6 all-to-all-start.1
  375.5 96.4 %all-gather.3 = bf16[32,48,16]{1,2,0:T(8,128)(2,1)S(1)} all-gather(bf16[1,48,16]{1,2,0:T(8,128)(2,1)S(1)} %bitcast.239), channel_id=1, replica_groups=mesh['dp'=2,'expert'=16] {'dp','expert'}, dimensions={0}, use_global_device_ids=true | all-gather | bytes 50688 | tf_op jit(solution)/shard_map/all_gather | solution.py:115
  526.5 86.1 %all_to_all.20 = bf16[16,72,1536]{2,1,0:T(8,128)(2,1)S(1)} all-to-all(bf16[16,72,1536]{2,1,0:T(8,128)(2,1)S(1)} %multiply_convert_fusion), channel_id=1, replica_groups=mesh['dp'=2,'expert'=16] {'expert'}, dimensions={0} | all-to-all | bytes 7077888 | tf_op jit(solution)/shard_map/all_to_all | solution.py:269
  621.7 6.1 all-to-all-start.3
  627.9 72.5 %all-to-all-done.3 = bf16[16,72,1536]{2,1,0:T(8,128)(2,1)} async-done(((bf16[16,72,1536]{2,1,0:T(8,128)(2,1)}), bf16[16,72,1536]{2,1,0:T(8,128)(2,1)}, u32[]{:S(2)}, u32[]{:S(2)}) %all-to-all-start.3) | async-done | bytes 3538976 | tf_op jit(solution)/shard_map/all_to_all | solution.py:286
  700.4 17.1 %scatter_custom_fusion.3 = f32[129,1536]{1,0:T(8,128)S(1)} fusion(s32[1152]{0:T(1024)S(1)} %get-tuple-element.180, bf16[1152,1536]{1,0:T(8,128)(2,1)} %bitcast.83, f32[]{:T(128)} %constant.83.clone.1), kind=kCustom, calls=%fused_computation.18 | custom fusion | flops 3538944 | bytes 4331524 | tf_op jit(solution)/shard_map/scatter-add | solution.py:304
  786.2 78.9 %reduce-scatter.35.cloned.1.call-done = f32[48,16]{1,0:T(8,128)} async-done(((f32[1536,16]{1,0:T(8,128)}), f32[48,16]{1,0:T(8,128)}) %reduce-scatter.35.cloned.1.call-update) | async-done | bytes 3088
  866.4 26.8 %reduce-scatter.29.cloned.1.call-done = bf16[512,768]{1,0:T(8,128)(2,1)} async-done(((bf16[512,1536]{1,0:T(8,128)(2,1)}), bf16[512,768]{1,0:T(8,128)(2,1)}) %reduce-scatter.29.cloned.1.call-update) | async-done | bytes 786448 | tf_op jit(solution)/shard_map/reduce_scatter | solution.py:300
  895.6 26.4 %reduce-scatter.27.cloned.1.call-done = bf16[768,512]{1,0:T(8,128)(2,1)} async-done(((bf16[1536,512]{1,0:T(8,128)(2,1)}), bf16[768,512]{1,0:T(8,128)(2,1)}) %reduce-scatter.27.cloned.1.call-update) | async-done | bytes 786448 | tf_op jit(solution)/shard_map/reduce_scatter | solution.py:297
  924.5 26.2 %reduce-scatter.25.cloned.1.call-done = bf16[768,512]{1,0:T(8,128)(2,1)} async-done(((bf16[1536,512]{1,0:T(8,128)(2,1)}), bf16[768,512]{1,0:T(8,128)(2,1)}) %reduce-scatter.25.cloned.1.call-update) | async-done | bytes 786448 | tf_op jit(solution)/shard_map/reduce_scatter | solution.py:294
  958.9 38.5 %all-reduce.7 = (f32[1536]{0:T(1024)S(1)}, f32[1536]{0:T(1024)S(1)}) all-reduce(f32[1536]{0:T(1024)S(1)} %get-tuple-element.107, f32[1536]{0:T(1024)S(1)} %copy-done.46), channel_id=7, replica_groups=mesh['dp'=2,'expert'=16] {'dp','expert'}, use_global_device_ids=true, to_apply=%region_33.34.clone | all-reduce | flops 3072 | bytes 24576
  999.6 58.6 %reduce-scatter.21.cloned.1.call-done = f32[48,512]{1,0:T(8,128)} async-done(((f32[1536,512]{1,0:T(8,128)}), f32[48,512]{1,0:T(8,128)}) %reduce-scatter.21.cloned.1.call-update) | async-done | bytes 98320 | tf_op jit(solution)/shard_map/reduce_scatter | solution.py:407
  1058.2 107.3 %reduce-scatter.19.cloned.1.call-done = f32[48,512]{1,0:T(8,128)} async-done(((f32[1536,512]{1,0:T(8,128)}), f32[48,512]{1,0:T(8,128)}) %reduce-scatter.19.cloned.1.call-update) | async-done | bytes 98320 | tf_op jit(solution)/shard_map/reduce_scatter | solution.py:406
  1165.5 142.0 %reduce-scatter.23.cloned.1.call-done = f32[48,1536]{1,0:T(8,128)} async-done(((f32[1536,1536]{1,0:T(8,128)}), f32[48,1536]{1,0:T(8,128)}) %reduce-scatter.23.cloned.1.call-update) | async-done | bytes 294928 | tf_op jit(solution)/shard_map/reduce_scatter | solution.py:408
  1307.5 140.9 %reduce-scatter.17.cloned.1.call-done = f32[48,1536]{1,0:T(8,128)} async-done(((f32[1536,1536]{1,0:T(8,128)}), f32[48,1536]{1,0:T(8,128)}) %reduce-scatter.17.cloned.1.call-update) | async-done | bytes 294928 | tf_op jit(solution)/shard_map/reduce_scatter | solution.py:405
  (300 shorter events, 217.5 us)
Async XLA Ops:
  8.0 63.8 %all-gather.12.cloned.1.call-start = ((), (), s32[]{:S(2)}) async-start(), calls=%async_computation.14 | async-start | bytes 1622016 | tf_op jit(solution)/shard_map/all_gather | solution.py:112
  8.8 115.0 %all-gather.14.cloned.1.call-start = ((), (), s32[]{:S(2)}) async-start(), calls=%async_computation.15 | async-start | bytes 1622016 | tf_op jit(solution)/shard_map/all_gather | solution.py:111
  9.5 179.5 %all-gather.16.cloned.1.call-start = ((), (), s32[]{:S(2)}) async-start(), calls=%async_computation.16 | async-start | bytes 4866048 | tf_op jit(solution)/shard_map/all_gather | solution.py:110
  10.3 243.9 %all-gather.18.cloned.1.call-start = ((), (), s32[]{:S(2)}) async-start(), calls=%async_computation.17 | async-start | bytes 4866048 | tf_op jit(solution)/shard_map/all_gather | solution.py:113
  71.6 121.7 %copy-start.41 = (f32[128,32]{0,1:T(8,128)}, f32[128,32]{0,1:T(8,128)S(1)}, u32[]{:S(2)}) copy-start(f32[128,32]{0,1:T(8,128)S(1)} %get-tuple-element.190) | copy-start | bytes 49156
  71.6 121.7 %copy-start.43 = (f32[128,32]{0,1:T(8,128)}, f32[128,32]{0,1:T(8,128)S(1)}, u32[]{:S(2)}) copy-start(f32[128,32]{0,1:T(8,128)S(1)} %get-tuple-element.191) | copy-start | bytes 49156
  257.4 461.1 %copy-start.3 = (f32[128,1536]{1,0:T(8,128)}, f32[128,1536]{1,0:T(8,128)S(1)}, u32[]{:S(2)}) copy-start(f32[128,1536]{1,0:T(8,128)S(1)} %get-tuple-element.195) | copy-start | bytes 2359300
  257.5 220.8 %copy-start.10 = (bf16[128,1536]{1,0:T(8,128)(2,1)}, bf16[128,1536]{1,0:T(8,128)(2,1)S(1)}, u32[]{:S(2)}) copy-start(bf16[128,1536]{1,0:T(8,128)(2,1)S(1)} %multiply_convert_fusion.4) | copy-start | bytes 1179652
  262.9 78.6 %all-to-all-start = ((bf16[16,72,1536]{2,1,0:T(8,128)(2,1)}), bf16[16,72,1536]{2,1,0:T(8,128)(2,1)}, u32[]{:S(2)}, u32[]{:S(2)}) async-start(bf16[16,72,1536]{2,1,0:T(8,128)(2,1)} %bitcast.199), calls=%async_computation | async-start | bytes 7077888 | tf_op jit(solution)/shard_map/all_to_all | solution.py:228
  268.9 29.9 %all-gather.20.cloned.1.call-start = ((), (), s32[]{:S(2)}) async-start(), calls=%async_computation.25 | async-start | bytes 2359296 | tf_op jit(solution)/shard_map/all_gather | solution.py:118
  269.5 77.9 %all-gather.22.cloned.1.call-start = ((), (), s32[]{:S(2)}) async-start(), calls=%async_computation.26 | async-start | bytes 2359296 | tf_op jit(solution)/shard_map/all_gather | solution.py:119
  270.1 85.8 %all-gather.24.cloned.1.call-start = ((), (), s32[]{:S(2)}) async-start(), calls=%async_computation.27 | async-start | bytes 2359296 | tf_op jit(solution)/shard_map/all_gather | solution.py:120
  361.5 117.2 %all-to-all-start.1 = ((bf16[16,72,1536]{2,1,0:T(8,128)(2,1)}), bf16[16,72,1536]{2,1,0:T(8,128)(2,1)}, u32[]{:S(2)}, u32[]{:S(2)}) async-start(bf16[16,72,1536]{2,1,0:T(8,128)(2,1)} %bitcast.204), calls=%async_computation.1 | async-start | bytes 7077888 | tf_op jit(solution)/shard_map/all_to_all | solution.py:234
  621.7 78.7 %all-to-all-start.3 = ((bf16[16,72,1536]{2,1,0:T(8,128)(2,1)}), bf16[16,72,1536]{2,1,0:T(8,128)(2,1)}, u32[]{:S(2)}, u32[]{:S(2)}) async-start(bf16[16,72,1536]{2,1,0:T(8,128)(2,1)} %bitcast.205), calls=%async_computation.3 | async-start | bytes 7077888 | tf_op jit(solution)/shard_map/all_to_all | solution.py:286
  627.8 129.4 %reduce-scatter.33.cloned.1.call-start = ((), (), s32[]{:S(2)}) async-start(), calls=%async_computation.29 | async-start | bytes 393216
  733.6 31.7 %reduce-scatter.31.cloned.1.call-start = ((), (), s32[]{:S(2)}) async-start(), calls=%async_computation.28 | async-start | bytes 393216
  738.9 126.1 %reduce-scatter.35.cloned.1.call-start = ((), (), s32[]{:S(2)}) async-start(), calls=%async_computation.30 | async-start | bytes 811008
  740.2 153.0 %reduce-scatter.29.cloned.1.call-start = ((), (), s32[]{:S(2)}) async-start(), calls=%async_computation.24 | async-start | bytes 2359296 | tf_op jit(solution)/shard_map/reduce_scatter | solution.py:300
  745.8 176.2 %reduce-scatter.27.cloned.1.call-start = ((), (), s32[]{:S(2)}) async-start(), calls=%async_computation.23 | async-start | bytes 2359296 | tf_op jit(solution)/shard_map/reduce_scatter | solution.py:297
  751.6 199.1 %reduce-scatter.25.cloned.1.call-start = ((), (), s32[]{:S(2)}) async-start(), calls=%async_computation.22 | async-start | bytes 2359296 | tf_op jit(solution)/shard_map/reduce_scatter | solution.py:294
  757.1 301.1 %reduce-scatter.21.cloned.1.call-start = ((), (), s32[]{:S(2)}) async-start(), calls=%async_computation.20 | async-start | bytes 3244032 | tf_op jit(solution)/shard_map/reduce_scatter | solution.py:407
  760.5 405.0 %reduce-scatter.19.cloned.1.call-start = ((), (), s32[]{:S(2)}) async-start(), calls=%async_computation.19 | async-start | bytes 3244032 | tf_op jit(solution)/shard_map/reduce_scatter | solution.py:406
  768.9 538.6 %reduce-scatter.23.cloned.1.call-start = ((), (), s32[]{:S(2)}) async-start(), calls=%async_computation.21 | async-start | bytes 9732096 | tf_op jit(solution)/shard_map/reduce_scatter | solution.py:408
  774.0 674.4 %reduce-scatter.17.cloned.1.call-start = ((), (), s32[]{:S(2)}) async-start(), calls=%async_computation.18 | async-start | bytes 9732096 | tf_op jit(solution)/shard_map/reduce_scatter | solution.py:405
  (58 other events, 1288.9 us)
Sparse Core Ops, SparseCore 0:
  11.8 54.9 all-gather.11
  69.6 54.0 all-gather.13
  126.7 62.2 all-gather.15
  191.8 62.3 all-gather.17
Sparse Core Ops, SparseCore 1:
  270.9 27.9 all-gather.19
  300.2 27.0 all-gather.21
  328.7 27.0 all-gather.23
  733.6 17.1 reduce-scatter.32
  753.7 11.5 reduce-scatter.30
  770.4 94.6 reduce-scatter.34
  867.1 26.0 reduce-scatter.28
  896.0 25.9 reduce-scatter.26
  924.7 25.9 reduce-scatter.24
  957.6 100.5 reduce-scatter.20
  1065.0 100.5 reduce-scatter.18
  1173.0 134.4 reduce-scatter.22
  1313.8 134.5 reduce-scatter.16
where the time goes:
time: 1470 us; the launch traced here: 1460 us
  waiting for transfers between devices  919 us (63%)
  blocking collectives  272 us (19%)
  matrix products  91.5 us (6%)
  local copies, waits for them, and re-layouts  85.7 us (6%)
  other arithmetic  47.3 us (3%)
  starting transfers between devices  23.1 us (2%)
  between operations  17.2 us (1%)
    reduce_scatter x1, waiting for transfers between devices, body(): lax.psum_scatter(out_weight_grad, ('dp', 'expert'), scatter_dimension=0,...  142 us
    reduce_scatter x1, waiting for transfers between devices, body(): lax.psum_scatter(query_weight_grad, ('dp', 'expert'), scatter_dimension=0...  141 us
    reduce_scatter x1, waiting for transfers between devices, body(): lax.psum_scatter(key_weight_grad, ('dp', 'expert'), scatter_dimension=0,...  107 us
    all_gather x1, blocking collectives, body(): lax.all_gather(w_router, ('dp', 'expert'), axis=0, tiled=True)  96.4 us
    unnamed x20, waiting for transfers between devices  87.6 us
    all_to_all x1, blocking collectives, body(): lax.all_to_all(slot_grad, 'expert', split_axis=0, concat_axis=0, tiled=True)  86.1 us
    unnamed x2, blocking collectives  77.8 us
    all_to_all x1, waiting for transfers between devices, body(): lax.all_to_all(row_grad.reshape(owners, capacity, model_width), 'expert',...  72.5 us
  transfers between devices with their start and end apart: 20, of which 16 were waited for; matrix products, arithmetic and copies ran while one was open for 8% of the time, Pallas kernels for 0%

commit v1 on v0

--- a/solution.py
+++ b/solution.py
@@ -1,8 +1,11 @@
+import functools
 import math
 
 import jax
 import jax.numpy as jnp
 from jax import lax
+from jax.experimental import pallas as pl
+from jax.experimental.pallas import tpu as pltpu
 from jax.sharding import PartitionSpec as P
 
 HEAD_DIM = 64
@@ -87,7 +90,1029 @@
     return (pair_slot, slot_token[: experts * capacity])
 
 
-def body(
+MESH = pl.DeviceIdType.MESH
+BF16 = jnp.bfloat16
+F32 = jnp.float32
+NAR = 128
+
+
+def remote(src, dst, send_sem, recv_sem, device):
+    return pltpu.make_async_remote_copy(
+        src_ref=src,
+        dst_ref=dst,
+        send_sem=send_sem,
+        recv_sem=recv_sem,
+        device_id=device,
+        device_id_type=MESH,
+    )
+
+
+class Place:
+    def __init__(self):
+        self.i = lax.axis_index("dp")
+        self.e = lax.axis_index("expert")
+        self.a = self.e // 4
+        self.bc = self.e % 4
+        self.y = self.bc // 2
+        self.c = self.bc % 2
+
+    def over_x(self):
+        return (1 - self.i, self.e)
+
+    def over_y(self):
+        return (self.i, self.e + 2 - 4 * self.y)
+
+    def over_core(self):
+        return (self.i, self.e + 1 - 2 * self.c)
+
+    def order(self, k):
+        turn = (1 - 2 * k) * (1 - k // 2)
+        inner = (self.a * (3 - self.a)) // 2
+        half = self.a // 2
+        step = k + inner * turn
+        return step + half * (3 - 2 * step)
+
+    def barrier(self):
+        sem = pltpu.get_barrier_semaphore()
+        peers = [self.over_x(), self.over_y(), self.over_core()]
+        for shift in range(1, 4):
+            peers.append((self.i, ((self.a + shift) % 4) * 4 + self.bc))
+        for peer in peers:
+            pl.semaphore_signal(sem, inc=1, device_id=peer, device_id_type=MESH)
+        pl.semaphore_wait(sem, len(peers))
+
+
+class Gather:
+    SENDS = 20
+    RECVS = 16
+
+    def __init__(self, place, view, sends, recvs):
+        self.p, self.view, self.sends, self.recvs = place, view, sends, recvs
+
+    def copy(self, block, slot, device):
+        ref = self.view(block)
+        return remote(ref, ref, self.sends.at[slot], self.recvs.at[block], device)
+
+    def right(self, a1):
+        return self.copy(a1 * 4 + self.p.bc, a1, (self.p.i, self.p.e + 4))
+
+    def left(self, a1):
+        return self.copy(a1 * 4 + self.p.bc, 4 + a1, (self.p.i, self.p.e - 4))
+
+    def across(self, a1):
+        return self.copy(a1 * 4 + self.p.bc, 8 + a1, self.p.over_y())
+
+    def core(self, a1, y1):
+        return self.copy(a1 * 4 + y1 * 2 + self.p.c, 12 + a1 * 2 + y1, self.p.over_core())
+
+    def landed(self, block):
+        self.copy(block, 0, self.p.over_core()).wait_recv()
+
+    def begin(self):
+        p = self.p
+
+        @pl.when(p.a < 3)
+        def _():
+            self.right(p.a).start()
+
+        @pl.when(p.a > 0)
+        def _():
+            self.left(p.a).start()
+
+        self.across(p.a).start()
+        self.core(p.a, p.y).start()
+
+    def along(self, k):
+        p = self.p
+        a1 = p.order(k)
+        self.landed(a1 * 4 + p.bc)
+
+        @pl.when((a1 < p.a) & (p.a < 3))
+        def _():
+            self.right(a1).start()
+
+        @pl.when((a1 > p.a) & (p.a > 0))
+        def _():
+            self.left(a1).start()
+
+        self.across(a1).start()
+        self.core(a1, p.y).start()
+
+    def cross(self, k):
+        p = self.p
+        a1 = p.order(k)
+        self.landed(a1 * 4 + (1 - p.y) * 2 + p.c)
+        self.core(a1, 1 - p.y).start()
+
+    def join(self, k):
+        p = self.p
+        a1 = p.order(k)
+        self.landed(a1 * 4 + (1 - p.c))
+        self.landed(a1 * 4 + 2 + (1 - p.c))
+
+    def drain(self):
+        p = self.p
+        for a1 in range(4):
+
+            @pl.when((a1 <= p.a) & (p.a < 3))
+            def _():
+                self.right(a1).wait_send()
+
+            @pl.when((a1 >= p.a) & (p.a > 0))
+            def _():
+                self.left(a1).wait_send()
+
+            self.across(a1).wait_send()
+            self.core(a1, 0).wait_send()
+            self.core(a1, 1).wait_send()
+
+
+class Scatter:
+    SENDS = 16
+    RECVS = 16
+
+    def __init__(self, place, part, core_in, y_in, a_in, sends, recvs):
+        self.p, self.part = place, part
+        self.core_in, self.y_in, self.a_in = core_in, y_in, a_in
+        self.sends, self.recvs = sends, recvs
+
+    def to_core(self, a1, y1):
+        p = self.p
+        slot = a1 * 2 + y1
+        return remote(
+            self.part(a1, y1 * 2 + 1 - p.c),
+            self.core_in.at[a1, y1],
+            self.sends.at[slot],
+            self.recvs.at[slot],
+            p.over_core(),
+        )
+
+    def to_y(self, a1):
+        p = self.p
+        return remote(
+            self.part(a1, (1 - p.y) * 2 + p.c),
+            self.y_in.at[a1],
+            self.sends.at[8 + a1],
+            self.recvs.at[8 + a1],
+            p.over_y(),
+        )
+
+    def to_a(self, a1):
+        p = self.p
+        return remote(
+            self.part(a1, p.bc),
+            self.a_in.at[p.a],
+            self.sends.at[12 + a1],
+            self.recvs.at[12 + p.a],
+            (p.i, a1 * 4 + p.bc),
+        )
+
+    def from_a(self, a1):
+        p = self.p
+        return remote(
+            self.a_in.at[a1],
+            self.a_in.at[a1],
+            self.sends.at[12 + a1],
+            self.recvs.at[12 + a1],
+            (p.i, a1 * 4 + p.bc),
+        )
+
+    def start(self, a1):
+        self.to_core(a1, 0).start()
+        self.to_core(a1, 1).start()
+
+    def add(self, ref, other):
+        ref[...] = (ref[...].astype(F32) + other[...].astype(F32)).astype(ref.dtype)
+
+    def core(self, a1):
+        p = self.p
+        for y1 in range(2):
+            self.to_core(a1, y1).wait_recv()
+        self.add(self.part(a1, (1 - p.y) * 2 + p.c), self.core_in.at[a1, 1 - p.y])
+        self.to_y(a1).start()
+        self.add(self.part(a1, p.bc), self.core_in.at[a1, p.y])
+
+    def cross(self, a1):
+        p = self.p
+        self.to_y(a1).wait_recv()
+        self.add(self.part(a1, p.bc), self.y_in.at[a1])
+
+        @pl.when(a1 != p.a)
+        def _():
+            self.to_a(a1).start()
+
+        @pl.when(a1 == p.a)
+        def _():
+            self.a_in[a1] = self.part(a1, p.bc)[...]
+
+    def finish(self):
+        p = self.p
+        for a1 in range(4):
+
+            @pl.when(a1 != p.a)
+            def _():
+                self.from_a(a1).wait_recv()
+
+    def total(self):
+        return (
+            self.a_in[0].astype(F32)
+            + self.a_in[1].astype(F32)
+            + self.a_in[2].astype(F32)
+            + self.a_in[3].astype(F32)
+        )
+
+    def drain(self):
+        p = self.p
+        for a1 in range(4):
+            self.to_core(a1, 0).wait_send()
+            self.to_core(a1, 1).wait_send()
+            self.to_y(a1).wait_send()
+
+            @pl.when(a1 != p.a)
+            def _():
+                self.to_a(a1).wait_send()
+
+
+def lane_iota(shape):
+    return lax.broadcasted_iota(jnp.int32, shape, len(shape) - 1)
+
+
+def swap_halves(values):
+    lane = lane_iota(values.shape) % HEAD_DIM
+    half = HEAD_DIM // 2
+    return jnp.where(
+        lane < half,
+        pltpu.roll(values, values.shape[-1] - half, 1),
+        pltpu.roll(values, half, 1),
+    )
+
+
+def split_heads(tile):
+    low = lane_iota(tile.shape) < HEAD_DIM
+    turned = pltpu.roll(tile, HEAD_DIM, 1)
+    zero = jnp.zeros_like(tile)
+    return (
+        (jnp.where(low, tile, zero), jnp.where(low, zero, turned)),
+        (jnp.where(low, turned, zero), jnp.where(low, zero, tile)),
+    )
+
+
+def inverse_rms(values):
+    return lax.rsqrt(jnp.mean(values * values, axis=1, keepdims=True) + NORM_EPS)
+
+
+def gain_rows(narrow, experts):
+    shape = (16, narrow.shape[1])
+    row = lax.broadcasted_iota(jnp.int32, shape, 0)
+    pick = jnp.where(lane_iota(shape) == row + experts, 1.0, 0.0).astype(BF16)
+    return dot_last(pick, narrow)
+
+
+def front_kernel(
+    tok, wp, wo, cot, eg, eu, ed, cs, sn, vis, hit, kept,
+    w_out_all, wo_out_all, x_all, cot_all, egp, eup, edp, att_in, q_out, k_out, v_out, pr, att, hid, fe, gates,
+    w_all, wo_all, klo, khi, vlo, vhi, opart, orecv,
+    ga_s, ga_r, gb_s, gb_r, gw_s, gw_r, gc_s, gc_r, xs, xr, loc,
+):
+    p = Place()
+    i, e = p.i, p.e
+    rows = tok.shape[0]
+    depth = wo.shape[0]
+    plane = 16 * depth
+    q_width = q_out.shape[1]
+    k_width = k_out.shape[1]
+    experts = 16
+    wide = q_width + 2 * k_width
+
+    def w_row(ip, block):
+        return pl.ds(pl.multiple_of(ip * plane + block * depth, 16), depth)
+
+    def row_block(ip):
+        return pl.ds(pl.multiple_of(ip * rows, rows), rows)
+
+    p.barrier()
+    give_w = remote(wp.at[1 - i], w_all.at[w_row(i, e)], xs.at[0], xr.at[0], p.over_x())
+    give_w.start()
+    take_w = remote(w_all.at[w_row(1 - i, e)], w_all.at[w_row(1 - i, e)], xs.at[0], xr.at[0], p.over_x())
+    give_x = remote(tok, x_all.at[i], xs.at[1], xr.at[1], p.over_x())
+    take_x = remote(x_all.at[1 - i], x_all.at[1 - i], xs.at[1], xr.at[1], p.over_x())
+    give_x.start()
+
+    ga = Gather(p, lambda block: w_all.at[w_row(i, block)], ga_s, ga_r)
+    gb = Gather(p, lambda block: w_all.at[w_row(1 - i, block)], gb_s, gb_r)
+    gw = Gather(p, lambda block: wo_all.at[w_row(0, block)], gw_s, gw_r)
+    gc = Gather(
+        p, lambda block: cot_all.at[block // 4, pl.ds(pl.multiple_of((block % 4) * rows, rows), rows)], gc_s, gc_r
+    )
+
+    w_all[w_row(i, e), :] = wp[i]
+    ga.begin()
+    own_cot = pltpu.make_async_copy(cot, gc.view(e), loc.at[0])
+    own_cot.start()
+    wo_all[w_row(0, e), :] = wo[...]
+    x_all[i] = tok[...]
+    take_w.wait_recv()
+    gb.begin()
+    experts_out = [
+        remote(src, dst, xs.at[2 + n], xr.at[2 + n], p.over_x())
+        for n, (src, dst) in enumerate(((eg, egp), (eu, eup), (ed, edp)))
+    ]
+    for one in experts_out:
+        one.start()
+    for k in range(1, 4):
+        ga.along(k)
+        ga.cross(k - 1)
+        gb.along(k)
+        gb.cross(k - 1)
+    gw.begin()
+    ga.cross(3)
+    gb.cross(3)
+    own_cot.wait()
+    for k in range(4):
+        ga.join(k)
+        gb.join(k)
+
+    events = []
+    for k in range(1, 4):
+        events.append(functools.partial(gw.along, k))
+        events.append(functools.partial(gw.cross, k - 1))
+        if k == 1:
+            events.append(gc.begin)
+    events.append(functools.partial(gw.cross, 3))
+    late = []
+    for k in range(1, 4):
+        late.append(functools.partial(gc.along, k))
+        late.append(functools.partial(gc.cross, k - 1))
+    late.append(functools.partial(gc.cross, 3))
+
+    def serve():
+        if events:
+            events.pop(0)()
+
+    w_save = pltpu.make_async_copy(w_all, w_out_all, loc.at[1])
+    w_save.start()
+    take_x.wait_recv()
+    narrow = w_all[:, wide:]
+    gains = gain_rows(narrow, experts)
+    for ip in range(2):
+        x = x_all[ip].astype(F32)
+        att_in[ip * rows : (ip + 1) * rows, :] = (x * inverse_rms(x) * gains[0:1]).astype(BF16)
+    serve()
+    cos, sin = cs[...], sn[...]
+
+    def rope(values):
+        return values * cos + swap_halves(values) * sin
+
+    for tile in range(wide // 256):
+        lin = dot_plain(att_in[...], w_all[:, tile * 256 : (tile + 1) * 256])
+        for half in range(2):
+            col = tile * 256 + half * 128
+            part = lin[:, half * 128 : (half + 1) * 128]
+            if col < q_width:
+                q_out[:, col : col + 128] = rope(part).astype(BF16)
+            elif col < q_width + k_width:
+                turned = rope(part)
+                n = (col - q_width) // 128
+                k_out[:, n * 128 : (n + 1) * 128] = turned.astype(BF16)
+                for g, (low, high) in enumerate(split_heads(turned)):
+                    klo[2 * n + g] = low.astype(BF16)
+                    khi[2 * n + g] = high.astype(BF16)
+            else:
+                n = (col - q_width - k_width) // 128
+                v_out[:, n * 128 : (n + 1) * 128] = part.astype(BF16)
+                for g, (low, high) in enumerate(split_heads(part)):
+                    vlo[2 * n + g] = low.astype(BF16)
+                    vhi[2 * n + g] = high.astype(BF16)
+    serve()
+    ratio = q_width // k_width
+    scale = HEAD_DIM**-0.5
+    for pair in range(q_width // 128):
+        lanes = slice(pair * 128, (pair + 1) * 128)
+        out = None
+        for side, (keys, vals) in enumerate(((klo, vlo), (khi, vhi))):
+            head = 2 * pair + side
+            g = head // ratio
+            scores = dot_last(q_out[:, lanes], keys[g]) * scale
+            scores = jnp.where(vis[...] > 0, scores, MASK_FILL)
+            top = jnp.max(scores, axis=1, keepdims=True)
+            grown = jnp.exp(scores - top)
+            probs = grown / jnp.sum(grown, axis=1, keepdims=True)
+            pr[head] = probs
+            term = dot_plain(probs.astype(BF16), vals[g])
+            out = term if out is None else out + term
+        att[:, lanes] = out.astype(BF16)
+        serve()
+    while events:
+        serve()
+    for k in range(4):
+        gw.join(k)
+    wo_save = pltpu.make_async_copy(wo_all, wo_out_all, loc.at[2])
+    wo_save.start()
+    opart[...] = dot_plain(att[row_block(1 - i), :], wo_all[...]).astype(BF16)
+    give_o = remote(opart, orecv, xs.at[5], xr.at[5], p.over_x())
+    give_o.start()
+    hid[...] = tok[...].astype(F32) + dot_plain(att[row_block(i), :], wo_all[...])
+    late[0]()
+    late[1]()
+    give_o.wait_recv()
+    state = hid[...] + orecv[...].astype(F32)
+    hid[...] = state
+    ffn_in = (state * inverse_rms(state) * gains[1:2]).astype(BF16)
+    width = ffn_in.shape[1]
+    fe[:, :width] = ffn_in
+    logits = dot_plain(ffn_in, narrow)
+    chosen = hit[...] > 0
+    logits = jnp.where(chosen, logits, MASK_FILL)
+    grown = jnp.where(chosen, jnp.exp(logits - jnp.max(logits, axis=1, keepdims=True)), 0.0)
+    gate = grown / jnp.sum(grown, axis=1, keepdims=True)
+    gates[...] = gate
+    gate = gate * kept[...]
+    gate_high = gate.astype(BF16).astype(F32)
+    fe[:, width:] = (gate_high + pltpu.roll(gate - gate_high, experts, 1)).astype(BF16)
+    for one in late[2:]:
+        one()
+    for k in range(4):
+        gc.join(k)
+    for one in experts_out:
+        one.wait()
+    for one in (give_w, give_x, give_o):
+        one.wait_send()
+    for g in (ga, gb, gw, gc):
+        g.drain()
+    w_save.wait()
+    wo_save.wait()
+
+
+def middle_kernel(
+    fe, cot_all, eg, eu, ed, egp, eup, edp,
+    total, mixp, og_own, ou_own, od_own, og_peer, ou_peer, od_peer,
+    f_all, part, core_in, y_in, a_in, wg, wu, wd, cot, og, h1, h2, hidden, gp, up, mix, dg, du, dd,
+    ga_s, ga_r, sc_s, sc_r, loc, cot_sem, mix_sem,
+):
+    p = Place()
+    i, e = p.i, p.e
+    rows = fe.shape[0]
+    width = og.shape[1]
+    half = width // 2
+    experts = 16
+    f_all[p.a, pl.ds(pl.multiple_of(p.bc * rows, rows), rows), :] = fe[...]
+    p.barrier()
+    g = Gather(p, lambda block: f_all.at[block // 4, pl.ds(pl.multiple_of((block % 4) * rows, rows), rows)], ga_s, ga_r)
+    g.begin()
+
+    def half_rows(ip):
+        return pl.ds(pl.multiple_of(ip * half, half), half)
+
+    loads = []
+    for ip, (a1, a2, a3) in ((i, (eg, eu, ed)), (1 - i, (egp, eup, edp))):
+        loads.append((a1, wg.at[half_rows(ip)]))
+        loads.append((a2, wu.at[half_rows(ip)]))
+        loads.append((a3, wd.at[:, half_rows(ip)]))
+    loads = [pltpu.make_async_copy(src, dst, loc.at[n]) for n, (src, dst) in enumerate(loads)]
+    for one in loads:
+        one.start()
+
+    def fetch(k):
+        a1 = p.order(k)
+        return pltpu.make_async_copy(cot_all.at[a1], cot.at[k % 2], cot_sem.at[k % 2])
+
+    def store_mix(a1):
+        return pltpu.make_async_copy(mix, mixp.at[a1], mix_sem)
+
+    fetch(0).start()
+    for ref in (dg, du, dd):
+        ref[...] = jnp.zeros_like(ref)
+    g.cross(0)
+    for one in loads:
+        one.wait()
+    sc = Scatter(
+        p,
+        lambda a1, b1: part.at[a1, pl.ds(pl.multiple_of(b1 * rows, rows), rows)],
+        core_in, y_in, a_in, sc_s, sc_r,
+    )
+
+    @pl.loop(0, 4)
+    def _(k):
+        a1 = p.order(k)
+        more = k < 3
+
+        @pl.when(more)
+        def _():
+            fetch(k + 1).start()
+
+        g.join(k)
+        f = f_all.at[a1]
+        h1[...] = dot_plain(f[:, :width], wg[...])
+        h2[...] = dot_plain(f[:, :width], wu[...])
+
+        @pl.when(more)
+        def _():
+            g.along(k + 1)
+
+        fetch(k).wait()
+        c = cot.at[k % 2]
+        meta = f[:, width:].astype(F32)
+        lane = lane_iota(meta.shape)
+        gate = jnp.sum(jnp.where((lane == e) | (lane == e + experts), meta, 0.0), axis=1, keepdims=True)
+        og[...] = (gate * c[...].astype(F32)).astype(BF16)
+        hg = dot_last(og[...], wd[...])
+        s = jax.nn.sigmoid(h1[...])
+        gp[...] = (hg * h2[...] * s * (1.0 + h1[...] * (1.0 - s))).astype(BF16)
+        up[...] = (hg * (h1[...] * s)).astype(BF16)
+        hidden[...] = (h1[...] * s * h2[...]).astype(BF16)
+
+        @pl.loop(0, 3)
+        def _(n):
+            cols = pl.ds(pl.multiple_of(n * 512, 512), 512)
+            part[a1, :, cols] = (dot_last(gp[...], wg[cols, :]) + dot_last(up[...], wu[cols, :])).astype(BF16)
+
+        @pl.when(k > 0)
+        def _():
+            store_mix(p.order(k - 1)).wait()
+
+        def project(n, gate_grad):
+            cols = pl.ds(pl.multiple_of(n * 512, 512), 512)
+            out = dot_plain(hidden[...], wd[:, cols]).astype(BF16).astype(F32)
+            mix[:, cols] = (gate * out).astype(BF16)
+            return gate_grad + jnp.sum(out * c[:, cols].astype(F32), axis=1, keepdims=True)
+
+        gate_grad = lax.fori_loop(0, 3, project, jnp.zeros((4 * rows, 1), F32))
+        store_mix(a1).start()
+        high = gate_grad.astype(BF16).astype(F32)
+        part[a1, :, width:] = jnp.where(
+            lane == e, high, jnp.where(lane == e + experts, gate_grad - high, 0.0)
+        ).astype(BF16)
+        sc.start(a1)
+
+        @pl.when(more)
+        def _():
+            g.cross(k + 1)
+
+        @pl.loop(0, 3)
+        def _(n):
+            cols = pl.ds(pl.multiple_of(n * 512, 512), 512)
+            dg[cols, :] += dot_first(f[:, cols], gp[...])
+            du[cols, :] += dot_first(f[:, cols], up[...])
+            dd[:, cols] += dot_first(hidden[...], og[:, cols])
+
+        sc.core(a1)
+
+        @pl.when(k > 0)
+        def _():
+            sc.cross(p.order(k - 1))
+
+    outs = [
+        (dg.at[half_rows(i)], og_own),
+        (du.at[half_rows(i)], ou_own),
+        (dd.at[:, half_rows(i)], od_own),
+    ]
+    outs = [pltpu.make_async_copy(src, dst, loc.at[n]) for n, (src, dst) in enumerate(outs)]
+    for one in outs:
+        one.start()
+    og_peer[...] = dg[half_rows(1 - i), :].astype(BF16)
+    ou_peer[...] = du[half_rows(1 - i), :].astype(BF16)
+    od_peer[...] = dd[:, half_rows(1 - i)].astype(BF16)
+    sc.cross(p.order(3))
+    sc.finish()
+    total[...] = sc.total()
+    store_mix(p.order(3)).wait()
+    for one in outs:
+        one.wait()
+    g.drain()
+    sc.drain()
+
+
+def back_kernel(
+    total, mixp, og_peer, ou_peer, od_peer, w_in, wo_in, x_all, att_in, q, kk, vv, pr, att, hid, gates, kept, cot, cs, sn,
+    out, tok_grad, dq_out, dk_out, dv_out, dwo_out, gains_out, egr, eur, edr,
+    w_all, wo_all, klo, khi, vlo, vhi, bg, ag, dq, dk, dv, apart, asend, arecv, state,
+    mpart, m_core, m_y, m_a, opart, o_core, o_y, o_a, wpart, w_core, w_y, w_a, wsend, wrecv,
+    sm_s, sm_r, so_s, so_r, sw_s, sw_r, xs, xr, loc,
+):
+    p = Place()
+    i, e = p.i, p.e
+    rows = cot.shape[0]
+    width = cot.shape[1]
+    q_width, k_width = q.shape[1], kk.shape[1]
+    wide = q_width + 2 * k_width
+    depth = dq_out.shape[0]
+    plane = 16 * depth
+    experts = 16
+    ratio = q_width // k_width
+    scale = HEAD_DIM**-0.5
+
+    def row_block(ip):
+        return pl.ds(pl.multiple_of(ip * rows, rows), rows)
+
+    load_mix = [pltpu.make_async_copy(mixp.at[a1], mpart.at[a1], loc.at[2 + a1]) for a1 in range(4)]
+    for one in load_mix:
+        one.start()
+    load_w = pltpu.make_async_copy(w_in, w_all, loc.at[0])
+    load_wo = pltpu.make_async_copy(wo_in, wo_all, loc.at[1])
+    load_w.start()
+    load_wo.start()
+    p.barrier()
+    sm = Scatter(p, lambda a1, b1: mpart.at[a1, row_block(b1)], m_core, m_y, m_a, sm_s, sm_r)
+    so = Scatter(
+        p,
+        lambda a1, b1: opart.at[pl.ds(pl.multiple_of((a1 * 4 + b1) * depth, 16), depth)],
+        o_core, o_y, o_a, so_s, so_r,
+    )
+    sw = Scatter(
+        p,
+        lambda a1, b1: wpart.at[:, pl.ds(pl.multiple_of((a1 * 4 + b1) * depth, 16), depth)],
+        w_core, w_y, w_a, sw_s, sw_r,
+    )
+    for a1 in range(4):
+        load_mix[a1].wait()
+        sm.start(a1)
+
+    load_w.wait()
+    narrow = w_all[:, wide:]
+    gains = gain_rows(narrow, experts)
+    lane = lane_iota((rows, NAR))
+    meta = total[:, width:]
+    gate_grad = (meta + pltpu.roll(meta, NAR - experts, 1)) * kept[...]
+    gate = gates[...]
+    logit_grad = (gate * (gate_grad - jnp.sum(gate * gate_grad, axis=1, keepdims=True))).astype(BF16)
+    ffn_grad = total[:, :width] + dot_last(logit_grad, narrow)
+    hidden = hid[...]
+    r2 = inverse_rms(hidden)
+    n2 = hidden * r2
+    ffn_in = (n2 * gains[1:2]).astype(BF16)
+    d2 = ffn_grad * gains[1:2]
+    state[...] = cot[...].astype(F32) + r2 * (d2 - n2 * jnp.mean(d2 * n2, axis=1, keepdims=True))
+    branch = state[...].astype(BF16)
+    bg[row_block(i), :] = branch
+    give_b = remote(bg.at[row_block(i)], bg.at[row_block(i)], xs.at[0], xr.at[0], p.over_x())
+    take_b = remote(bg.at[row_block(1 - i)], bg.at[row_block(1 - i)], xs.at[0], xr.at[0], p.over_x())
+    give_b.start()
+    ones = jnp.where(lane == experts + 1, 1.0, 0.0).astype(BF16)
+    gain_term = ffn_grad * n2
+    gain_high = gain_term.astype(BF16)
+    gain_low = (gain_term - gain_high.astype(F32)).astype(BF16)
+    small = dot_first(ffn_in, logit_grad) + dot_first(gain_high, ones) + dot_first(gain_low, ones)
+    small_ref = apart
+    small_ref[...] = small
+    for a1 in range(4):
+        sm.core(a1)
+
+    for n in range(k_width // 128):
+        for (tile, los, his) in ((kk, klo, khi), (vv, vlo, vhi)):
+            for g, (low, high) in enumerate(split_heads(tile[:, n * 128 : (n + 1) * 128].astype(F32))):
+                los[2 * n + g] = low.astype(BF16)
+                his[2 * n + g] = high.astype(BF16)
+    dk[...] = jnp.zeros_like(dk)
+    dv[...] = jnp.zeros_like(dv)
+    cos, sin = cs[...], sn[...]
+    low_lane = lane_iota((2 * rows, 128)) < HEAD_DIM
+
+    def unrope(values):
+        return values * cos - swap_halves(values) * sin
+
+    load_wo.wait()
+    take_b.wait_recv()
+    experts_out = [
+        remote(src, dst, xs.at[2 + n], xr.at[2 + n], p.over_x())
+        for n, (src, dst) in enumerate(((og_peer, egr), (ou_peer, eur), (od_peer, edr)))
+    ]
+    for one in experts_out:
+        one.start()
+    for n in range(q_width // 256):
+        lanes = slice(n * 256, (n + 1) * 256)
+        ag[:, lanes] = dot_last(bg[...], wo_all[lanes, :]).astype(BF16)
+    for n in range(q_width // 256):
+        lanes = slice(n * 256, (n + 1) * 256)
+        opart[lanes, :] = dot_first(att[:, lanes], bg[...]).astype(BF16)
+    for a1 in range(4):
+        so.start(a1)
+    for a1 in range(4):
+        sm.cross(a1)
+
+    for pair in range(q_width // 128):
+        lanes = slice(pair * 128, (pair + 1) * 128)
+        grad_in = ag[:, lanes]
+        q_pair = q[:, lanes]
+        q_grad = None
+        for side, (keys, vals) in enumerate(((klo, vlo), (khi, vhi))):
+            head = 2 * pair + side
+            g = head // ratio
+            probs = pr[head]
+            prob_grad = dot_last(grad_in, vals[g])
+            shift = jnp.sum(probs * prob_grad, axis=1, keepdims=True)
+            score_grad = (probs * (prob_grad - shift)).astype(BF16)
+            term = dot_plain(score_grad, keys[g])
+            q_grad = term if q_grad is None else q_grad + term
+            mine = low_lane if side == 0 else jnp.logical_not(low_lane)
+            k_term = jnp.where(mine, dot_first(score_grad, q_pair), 0.0)
+            v_term = jnp.where(mine, dot_first(probs.astype(BF16), grad_in), 0.0)
+            if g % 2 != side:
+                k_term = pltpu.roll(k_term, HEAD_DIM, 1)
+                v_term = pltpu.roll(v_term, HEAD_DIM, 1)
+            tile = slice((g // 2) * 128, (g // 2 + 1) * 128)
+            dk[:, tile] += k_term
+            dv[:, tile] += v_term
+        dq[:, lanes] = unrope(scale * q_grad).astype(BF16)
+        if pair < 4:
+            so.core(pair)
+    for n in range(k_width // 128):
+        lanes = slice(n * 128, (n + 1) * 128)
+        dq[:, q_width + n * 128 : q_width + (n + 1) * 128] = unrope(scale * dk[:, lanes]).astype(BF16)
+        dq[:, q_width + k_width + n * 128 : q_width + k_width + (n + 1) * 128] = dv[:, lanes].astype(BF16)
+    for a1 in range(4):
+        so.cross(a1)
+
+    back = [None, None]
+    for first in range(2):
+        ip = 1 - i if first == 0 else i
+        part = dot_last(dq[row_block(ip), :], w_all[:, :wide])
+        x = x_all[ip].astype(F32)
+        term = part * (x * inverse_rms(x))
+        high = term.astype(BF16)
+        low = (term - high.astype(F32)).astype(BF16)
+        pick = jnp.where(lane == experts, 1.0, 0.0).astype(BF16)
+        small_ref[...] += dot_first(high, pick) + dot_first(low, pick)
+        if first == 0:
+            asend[...] = part.astype(BF16)
+            give_a = remote(asend, arecv, xs.at[1], xr.at[1], p.over_x())
+            give_a.start()
+        else:
+            back = part
+    for ip in range(2):
+        for n in range(plane // 256):
+            block = slice(n * 256, (n + 1) * 256)
+            lanes = slice(ip * plane + n * 256, ip * plane + (n + 1) * 256)
+            wpart[ip, block, :wide] = dot_first(att_in[:, lanes], dq[...]).astype(BF16)
+        wpart[ip, :, wide:] = small_ref[ip * plane : (ip + 1) * plane, :].astype(BF16)
+    for a1 in range(4):
+        sw.start(a1)
+    give_a.wait_recv()
+    attn_grad = back + arecv[...].astype(F32)
+    x = x_all[i].astype(F32)
+    r1 = inverse_rms(x)
+    n1 = x * r1
+    d1 = attn_grad * gains[0:1]
+    tok_grad[...] = (state[...] + r1 * (d1 - n1 * jnp.mean(d1 * n1, axis=1, keepdims=True))).astype(BF16)
+    for a1 in range(4):
+        sw.core(a1)
+    sm.finish()
+    out[...] = (hidden + sm.total()).astype(BF16)
+    so.finish()
+    dwo_out[...] = so.total()
+    for a1 in range(4):
+        sw.cross(a1)
+    sw.finish()
+    summed = sw.total()
+    wsend[...] = summed
+    give_s = remote(wsend.at[1 - i], wrecv, xs.at[5], xr.at[5], p.over_x())
+    give_s.start()
+
+    def place_half(ip, values):
+        dq_out[:, pl.ds(pl.multiple_of(ip * q_width, 128), q_width)] = values[:, :q_width]
+        dk_out[:, pl.ds(pl.multiple_of(ip * k_width, 128), k_width)] = values[:, q_width : q_width + k_width]
+        dv_out[:, pl.ds(pl.multiple_of(ip * k_width, 128), k_width)] = values[:, q_width + k_width : wide]
+
+    mine = wsend[i]
+    place_half(i, mine)
+    give_s.wait_recv()
+    theirs = wrecv[...]
+    place_half(1 - i, theirs)
+    gains_out[...] = mine[:, wide:] + theirs[:, wide:]
+    for one in experts_out:
+        one.wait()
+    for one in (give_b, give_a, give_s):
+        one.wait_send()
+    for s in (sm, so, sw):
+        s.drain()
+
+
+def paired_body(
+    tokens, cotangent, norm_attn, w_query, key_projection, value_projection, w_out, norm_ffn, w_router,
+    expert_gate, expert_up, expert_down, routes, slot_order, doc_lengths, deal,
+):
+    rows, width = tokens.shape
+    depth = w_query.shape[0]
+    top_count = routes.shape[1]
+    experts = 16
+    capacity = 9 * rows * top_count // (8 * experts)
+    q_width = w_query.shape[1] // 2
+    k_width = key_projection.shape[1] // 2
+    wide = q_width + 2 * k_width
+    ff = expert_gate.shape[2]
+    half = width // 2
+    vm = pl.BlockSpec(memory_space=pltpu.VMEM)
+    hb = pl.BlockSpec(memory_space=pl.ANY)
+
+    def shaped(*dims, dtype=BF16):
+        return jax.ShapeDtypeStruct(dims, dtype)
+
+    def sems(n):
+        return pltpu.SemaphoreType.DMA((n,))
+
+    narrow = jnp.concatenate(
+        [w_router, norm_attn[:, None], norm_ffn[:, None], jnp.zeros((depth, NAR - experts - 2), BF16)], axis=1
+    )
+    packed = jnp.stack(
+        [
+            jnp.concatenate(
+                [
+                    w_query[:, h * q_width : (h + 1) * q_width],
+                    key_projection[:, h * k_width : (h + 1) * k_width],
+                    value_projection[:, h * k_width : (h + 1) * k_width],
+                    narrow,
+                ],
+                axis=1,
+            )
+            for h in range(2)
+        ]
+    )
+    group_places = deal[:, 0, :].reshape(-1)
+    group_docs, group_offsets = doc_layout(doc_lengths[0], group_places)
+    cosine, sine = rope_tables(group_offsets, HEAD_DIM)
+    cs = jnp.concatenate([cosine] * 4, axis=1)
+    sn = jnp.concatenate([-sine, sine, -sine, sine], axis=1)
+    vis = (
+        (group_docs[:, None] == group_docs[None, :]) & (group_places[:, None] >= group_places[None, :])
+    ).astype(F32)
+    pairs = rows * top_count
+    number = jnp.arange(pairs, dtype=jnp.int32)
+    taken_at = jnp.sum(
+        jnp.where(slot_order[0][None, :] == number[:, None], number[None, :], 0), axis=1
+    ).reshape(rows, top_count)
+    names = jnp.arange(experts, dtype=jnp.int32)
+    match = routes[:, :, None] == names[None, None, :]
+    hit = jnp.any(match, axis=1)
+    when = jnp.sum(jnp.where(match, taken_at[:, :, None], 0), axis=1)
+    rank = jnp.sum((hit[None, :, :] & (when[None, :, :] < when[:, None, :])).astype(jnp.int32), axis=1)
+    kept = hit & (rank < capacity)
+    pad = ((0, 0), (0, NAR - experts))
+    hit = jnp.pad(hit.astype(F32), pad)
+    kept = jnp.pad(kept.astype(F32), pad)
+
+    heads = q_width // HEAD_DIM
+    groups = k_width // HEAD_DIM
+    group_rows = 2 * rows
+    (w_all, wo_all, x_all, cot_all, egp, eup, edp, att_in, q, kk, vv, pr, att, hid, fe, gates) = pl.pallas_call(
+        front_kernel,
+        name="front",
+        out_shape=(
+            shaped(2 * 16 * depth, wide + NAR),
+            shaped(16 * depth, width),
+            shaped(2, rows, width),
+            shaped(4, 4 * rows, width),
+            shaped(half, ff),
+            shaped(half, ff),
+            shaped(ff, half),
+            shaped(group_rows, width),
+            shaped(group_rows, q_width),
+            shaped(group_rows, k_width),
+            shaped(group_rows, k_width),
+            shaped(heads, group_rows, group_rows, dtype=F32),
+            shaped(group_rows, q_width),
+            shaped(rows, width, dtype=F32),
+            shaped(rows, width + NAR),
+            shaped(rows, NAR, dtype=F32),
+        ),
+        in_specs=[vm, vm, vm, hb, hb, hb, hb, vm, vm, vm, vm, vm],
+        out_specs=(hb, hb, vm, hb, hb, hb, hb, vm, vm, vm, vm, vm, vm, vm, vm, vm),
+        scratch_shapes=[
+            pltpu.VMEM((2 * 16 * depth, wide + NAR), BF16),
+            pltpu.VMEM((16 * depth, width), BF16),
+            pltpu.VMEM((groups, group_rows, 128), BF16),
+            pltpu.VMEM((groups, group_rows, 128), BF16),
+            pltpu.VMEM((groups, group_rows, 128), BF16),
+            pltpu.VMEM((groups, group_rows, 128), BF16),
+            pltpu.VMEM((rows, width), BF16),
+            pltpu.VMEM((rows, width), BF16),
+        ]
+        + [sems(Gather.SENDS), sems(Gather.RECVS)] * 4
+        + [sems(6), sems(6), sems(3)],
+        compiler_params=pltpu.CompilerParams(collective_id=1, has_side_effects=True, vmem_limit_bytes=56 << 20),
+    )(
+        tokens, packed, w_out, cotangent, expert_gate[0], expert_up[0], expert_down[0], cs, sn, vis, hit, kept
+    )
+
+    (total, mixp, og_own, ou_own, od_own, og_peer, ou_peer, od_peer) = pl.pallas_call(
+        middle_kernel,
+        name="middle",
+        out_shape=(
+            shaped(rows, width + NAR, dtype=F32),
+            shaped(4, 4 * rows, width),
+            shaped(half, ff, dtype=F32),
+            shaped(half, ff, dtype=F32),
+            shaped(ff, half, dtype=F32),
+            shaped(half, ff),
+            shaped(half, ff),
+            shaped(ff, half),
+        ),
+        in_specs=[vm] + [hb] * 7,
+        out_specs=(vm, hb, hb, hb, hb, vm, vm, vm),
+        scratch_shapes=[
+            pltpu.VMEM((4, 4 * rows, width + NAR), BF16),
+            pltpu.VMEM((4, 4 * rows, width + NAR), BF16),
+            pltpu.VMEM((4, 2, rows, width + NAR), BF16),
+            pltpu.VMEM((4, rows, width + NAR), BF16),
+            pltpu.VMEM((4, rows, width + NAR), BF16),
+            pltpu.VMEM((width, ff), BF16),
+            pltpu.VMEM((width, ff), BF16),
+            pltpu.VMEM((ff, width), BF16),
+            pltpu.VMEM((2, 4 * rows, width), BF16),
+            pltpu.VMEM((4 * rows, width), BF16),
+            pltpu.VMEM((4 * rows, ff), F32),
+            pltpu.VMEM((4 * rows, ff), F32),
+            pltpu.VMEM((4 * rows, ff), BF16),
+            pltpu.VMEM((4 * rows, ff), BF16),
+            pltpu.VMEM((4 * rows, ff), BF16),
+            pltpu.VMEM((4 * rows, width), BF16),
+            pltpu.VMEM((width, ff), F32),
+            pltpu.VMEM((width, ff), F32),
+            pltpu.VMEM((ff, width), F32),
+            sems(Gather.SENDS),
+            sems(Gather.RECVS),
+            sems(Scatter.SENDS),
+            sems(Scatter.RECVS),
+            sems(6),
+            sems(2),
+            pltpu.SemaphoreType.DMA(()),
+        ],
+        compiler_params=pltpu.CompilerParams(collective_id=2, has_side_effects=True, vmem_limit_bytes=60 << 20),
+    )(fe, cot_all, expert_gate[0], expert_up[0], expert_down[0], egp, eup, edp)
+
+    def landing(block):
+        return [
+            pltpu.VMEM((4, 2) + block, BF16),
+            pltpu.VMEM((4,) + block, BF16),
+            pltpu.VMEM((4,) + block, BF16),
+        ]
+
+    (out, tok_grad, dq, dk, dv, dwo, gains, egr, eur, edr) = pl.pallas_call(
+        back_kernel,
+        name="back",
+        out_shape=(
+            shaped(rows, width),
+            shaped(rows, width),
+            shaped(depth, 2 * q_width, dtype=F32),
+            shaped(depth, 2 * k_width, dtype=F32),
+            shaped(depth, 2 * k_width, dtype=F32),
+            shaped(depth, width, dtype=F32),
+            shaped(depth, NAR, dtype=F32),
+            shaped(half, ff),
+            shaped(half, ff),
+            shaped(ff, half),
+        ),
+        in_specs=[vm, hb, hb, hb, hb, hb, hb] + [vm] * 13,
+        out_specs=(vm, vm, vm, vm, vm, vm, vm, hb, hb, hb),
+        scratch_shapes=[
+            pltpu.VMEM((2 * 16 * depth, wide + NAR), BF16),
+            pltpu.VMEM((16 * depth, width), BF16),
+            pltpu.VMEM((groups, group_rows, 128), BF16),
+            pltpu.VMEM((groups, group_rows, 128), BF16),
+            pltpu.VMEM((groups, group_rows, 128), BF16),
+            pltpu.VMEM((groups, group_rows, 128), BF16),
+            pltpu.VMEM((group_rows, width), BF16),
+            pltpu.VMEM((group_rows, q_width), BF16),
+            pltpu.VMEM((group_rows, wide), BF16),
+            pltpu.VMEM((group_rows, k_width), F32),
+            pltpu.VMEM((group_rows, k_width), F32),
+            pltpu.VMEM((2 * 16 * depth, NAR), F32),
+            pltpu.VMEM((rows, width), BF16),
+            pltpu.VMEM((rows, width), BF16),
+            pltpu.VMEM((rows, width), F32),
+            pltpu.VMEM((4, 4 * rows, width), BF16),
+        ]
+        + landing((rows, width))
+        + [pltpu.VMEM((16 * depth, width), BF16)]
+        + landing((depth, width))
+        + [pltpu.VMEM((2, 16 * depth, wide + NAR), BF16)]
+        + landing((2, depth, wide + NAR))
+        + [
+            pltpu.VMEM((2, depth, wide + NAR), F32),
+            pltpu.VMEM((depth, wide + NAR), F32),
+        ]
+        + [sems(Scatter.SENDS), sems(Scatter.RECVS)] * 3
+        + [sems(6), sems(6), sems(6)],
+        compiler_params=pltpu.CompilerParams(collective_id=3, has_side_effects=True, vmem_limit_bytes=60 << 20),
+    )(
+        total, mixp, og_peer, ou_peer, od_peer, w_all, wo_all, x_all, att_in, q, kk, vv, pr, att, hid, gates, kept,
+        cotangent, cs, sn,
+    )
+    return (
+        out,
+        tok_grad,
+        gains[:, experts],
+        dq,
+        dk,
+        dv,
+        dwo,
+        gains[:, experts + 1],
+        gains[:, :experts],
+        (og_own + egr.astype(F32))[None],
+        (ou_own + eur.astype(F32))[None],
+        (od_own + edr.astype(F32))[None],
+    )
+
+
+def general_body(
     tokens,
     cotangent,
     norm_attn,
@@ -458,4 +1483,6 @@
         P("expert", "dp", None),
         P("expert", None, "dp"),
     )
+    fast = mesh.shape["dp"] == 2 and mesh.shape["expert"] == 16
+    body = paired_body if fast else general_body
     return jax.shard_map(body, mesh=mesh, in_specs=in_specs, out_specs=out_specs, check_vma=False)

time: 1470 us -> 390 us (0.27)
  waiting for transfers between devices: 919 us -> 0 us
  Pallas kernels: 0 us -> 361 us
  blocking collectives: 272 us -> 0 us
  matrix products: 91.5 us -> 0 us
  local copies, waits for them, and re-layouts: 85.7 us -> 11 us
  other arithmetic: 47.3 us -> 17.3 us
  starting transfers between devices: 23.1 us -> 0 us
  between operations: 17.2 us -> 0.79 us
    reduce_scatter x7 -> x0, waiting for transfers between devices: 528 us -> none  [the longest x1 142 us: body(): lax.psum_scatter(out_weight_grad, ('dp', 'expert'), scatter_dimension=0,...]
    pallas_call x0 -> x3, Pallas kernels: none -> 361 us  [the longest x1 129 us: paired_body(): pl.pallas_call(middle_kernel, name='middle', out_shape=(shaped(rows, widt...]
    all_gather x7 -> x0, waiting for transfers between devices: 188 us -> none  [the longest x1 57.7 us: body(): lax.all_gather(w_out, ('dp', 'expert'), axis=0, tiled=True)]
    all_to_all x3 -> x0, waiting for transfers between devices: 115 us -> none  [the longest x1 72.5 us: body(): lax.all_to_all(row_grad.reshape(owners, capacity, model_width), 'expert',...]
    all_gather x3 -> x0, blocking collectives: 109 us -> none  [the longest x1 96.4 us: body(): lax.all_gather(w_router, ('dp', 'expert'), axis=0, tiled=True)]
    dot_general x29 -> x0, matrix products: 90.3 us -> none  [the longest x7 32.1 us: dot_first(): lax.dot_general(left_side, right_side, (((0,), (0,)), ((), ())), preferre...]
    unnamed x20 -> x0, waiting for transfers between devices: 87.6 us -> none
    all_to_all x1 -> x0, blocking collectives: 86.1 us -> none  [body(): lax.all_to_all(slot_grad, 'expert', split_axis=0, concat_axis=0, tiled=True)]
  transfers between devices with their start and end apart: 20 -> 0, of which waited for: 16 -> 0; matrix products, arithmetic and copies ran while one was open for 8% -> 0% of each run, Pallas kernels for 0% -> 0%
where the time goes in v1:
time: 390 us
  Pallas kernels  361 us (93%)
  other arithmetic  17.3 us (4%)
  local copies, waits for them, and re-layouts  11 us (3%)
    pallas_call x1, Pallas kernels, paired_body(): pl.pallas_call(middle_kernel, name='middle', out_shape=(shaped(rows, widt...  129 us
    pallas_call x1, Pallas kernels, paired_body(): pl.pallas_call(back_kernel, name='back', out_shape=(shaped(rows, width),...  123 us
    pallas_call x1, Pallas kernels, paired_body(): pl.pallas_call(front_kernel, name='front', out_shape=(shaped(2 * 16 * dep...  109 us

profile of v1, /device:TPU:24, one launch (start us, length us, event | category | flops | bytes accessed | tf_op | source)
XLA Modules:
  0.0 389.8 jit_solution(3328656075874589913)
XLA Ops:
  0.7 0.8 reduce-window.4
  2.2 0.8 convert_reduce_fusion.1
  3.7 0.7 fusion
  4.4 1.2 select_reduce_fusion
  5.6 0.8 copy.56
  6.3 0.8 copy.57
  7.1 0.8 copy.55
  8.1 0.7 select_reduce_fusion.1
  9.0 2.5 convert_reduce_fusion
  11.5 0.8 fusion.4
  13.0 0.9 fusion.3
  14.1 0.7 pad_maximum_fusion.wp
  14.9 0.8 and_convert_fusion.vis
  16.3 1.0 pad_maximum_fusion.1
  17.2 108.6 %front.1 = (bf16[1536,1408]{1,0:T(8,128)(2,1)}, bf16[768,1536]{1,0:T(8,128)(2,1)}, bf16[2,128,1536]{2,1,0:T(8,128)(2,1)}, bf16[4,512,1536]{2,1,0:T(8,128)(2,1)},...) custom-call(bf16[128,1536]{1,0:T(8,128)(2,1)} %tok.1, ...), custom_call_target="tpu_custom_call" | custom-call | tf_op jit(solution)/shard_map/front/pallas_call | solution.py:955
  125.9 128.9 %middle.1 = (f32[128,1664]{1,0:T(8,128)}, bf16[4,512,1536]{2,1,0:T(8,128)(2,1)}, f32[768,512]{1,0:T(8,128)}, f32[768,512]{1,0:T(8,128)}, f32[512,768]{1,0:T(8,12...) custom-call(bf16[128,1664]{1,0:T(8,128)(2,1)} %get-tuple-element.46.fe, ...), custom_call_target="tpu_custom_call" | custom-call | tf_op jit(solution)/shard_map/middle/pallas_call | solution.py:995
  254.8 123.2 %back.1 = (bf16[128,1536]{1,0:T(8,128)(2,1)}, bf16[128,1536]{1,0:T(8,128)(2,1)}, f32[48,1536]{1,0:T(8,128)}, f32[48,512]{1,0:T(8,128)}, f32[48,512]{1,0:T(8,128)...) custom-call(f32[128,1664]{1,0:T(8,128)} %get-tuple-element.51.total,, ...), custom_call_target="tpu_custom_call" | custom-call | tf_op jit(solution)/shard_map/back/pallas_call | solution.py:1048
  378.0 2.6 add_bitcast_fusion
  380.6 1.4 add_bitcast_fusion.1
  382.8 1.4 add_bitcast_fusion.2
  385.6 0.7 copy.74
  386.3 0.7 copy.75
  387.1 0.7 copy.76
  389.1 0.7 copy.79
  (44 shorter events, 6.7 us)
Async XLA Ops:
  0.6 14.2 %copy-start.12 = (s32[2,1,128]{2,1,0:T(1,128)S(1)}, s32[2,1,128]{2,1,0:T(1,128)}, u32[]{:S(2)}) copy-start(s32[2,1,128]{2,1,0:T(1,128)} %param.31) | copy-start | bytes 3076
  254.8 123.2 %copy-start.2 = (f32[512,768]{1,0:T(8,128)S(1)}, f32[512,768]{1,0:T(8,128)}, u32[]{:S(2)}) copy-start(f32[512,768]{1,0:T(8,128)} %get-tuple-element.78) | copy-start | bytes 4718596
  378.0 2.6 copy-start.1
  378.0 2.6 copy-start.4
  380.6 1.9 copy-start
  380.6 2.2 copy-start.3
  382.8 1.4 copy-start.9
  382.8 2.8 copy-start.6
  382.8 3.5 copy-start.5
  384.2 2.9 copy-start.8
  384.2 3.6 copy-start.11
  384.2 4.2 %copy-start.10 = (f32[48,512]{1,0:T(8,128)S(1)}, f32[48,512]{1,0:T(8,128)}, u32[]{:S(2)}) copy-start(f32[48,512]{1,0:T(8,128)} %get-tuple-element.162) | copy-start | bytes 294916
  384.2 4.9 %copy-start.7 = (f32[48,1536]{1,0:T(8,128)S(1)}, f32[48,1536]{1,0:T(8,128)}, u32[]{:S(2)}) copy-start(f32[48,1536]{1,0:T(8,128)} %get-tuple-element.163) | copy-start | bytes 884740
